TPU v7x, 256 devices: a whole 4x4x8 slice. The times are simulated.
256 devices in a mesh: seq: 64 (over z, x, core), head: 4 (over y).
Axes of the slice: x: 4, y: 4, z: 8, core: 2. Of those that a mesh axis runs over, the one named last changes fastest.
Arguments:
- queries: bfloat16 [131072, 8, 128], P('seq', 'head'), may hold values from -12.5 to 12.5
- key_rows_all_heads: bfloat16 [131072, 8, 128], P('seq', 'head'), may hold values from -12.5 to 12.5
- values: bfloat16 [131072, 8, 128], P('seq', 'head'), may hold values from -24 to 24
- output_gain: float32 [8, 128], P('head'), may hold values from 0.1 to 1.9
Outputs:
- normed_output: bfloat16 [131072, 8, 128], P('seq', 'head')
All inputs are finite; a program needn't handle non-finite values.
Results may differ from a plain program's by a relative error of at most 0.0087.
Values may be sent and summed in bfloat16 or wider, within the bound.
A program may use at most 64 MiB of HBM per device.

v0:
```python
import jax
import jax.numpy as jnp
from jax import lax
from jax.sharding import PartitionSpec as P

LANDMARKS = 512
NEWTON_STEPS = 2


epsilon = 1e-06


def softmax_last(scores):
    row_top = jnp.max(scores, axis=-1, keepdims=True)
    weights = jnp.exp(scores - row_top)
    return weights / jnp.sum(weights, axis=-1, keepdims=True)


def segment_averages(tokens_block, mark_count):
    row_count, head_count, feature_length = tokens_block.shape
    segment_length = row_count // mark_count
    summed = jnp.sum(
        tokens_block.reshape(mark_count, segment_length, head_count, feature_length),
        axis=1,
        dtype=jnp.float32,
    )
    return (summed / segment_length).astype(jnp.bfloat16)


def highest_product(first_factor, second_factor):
    return jnp.einsum("hij,hjk->hik", first_factor, second_factor, precision=lax.Precision.HIGHEST)


def newton_inverse(matrix, step_count):
    identity = jnp.eye(matrix.shape[-1], dtype=jnp.float32)
    magnitude = jnp.abs(matrix)
    column_top = jnp.max(jnp.sum(magnitude, axis=-2), axis=-1)
    row_top = jnp.max(jnp.sum(magnitude, axis=-1), axis=-1)
    inverse = jnp.swapaxes(matrix, -1, -2) / (column_top * row_top)[:, None, None]
    for repeat in range(step_count):
        product = highest_product(matrix, inverse)
        nested = highest_product(product, 7.0 * identity - product)
        nested = highest_product(product, 15.0 * identity - nested)
        inverse = highest_product(0.25 * inverse, 13.0 * identity - nested)
    return inverse


def on_device(queries, key_rows_all_heads, values, output_gain):
    marks_per_device = LANDMARKS // lax.axis_size("seq")
    score_scale = queries.shape[-1] ** (-0.5)
    query_marks = segment_averages(queries, marks_per_device)
    key_marks = segment_averages(key_rows_all_heads, marks_per_device)
    query_landmark_rows, key_landmark_rows = (
        lax.all_gather(query_marks, "seq", axis=0, tiled=True),
        lax.all_gather(key_marks, "seq", axis=0, tiled=True),
    )
    scores_b = (
        jnp.einsum(
            "nio,zio->inz",
            query_landmark_rows,
            key_rows_all_heads,
            preferred_element_type=jnp.float32,
        )
        * score_scale
    )
    local_top = jnp.max(scores_b, axis=-1)
    row_top = lax.pmax(local_top, "seq")
    landmark_weight_rows = jnp.exp(scores_b - row_top[:, :, None])
    local_total = jnp.sum(landmark_weight_rows, axis=-1)
    local_values = jnp.einsum(
        "jqo,ojw->jqw",
        landmark_weight_rows.astype(jnp.bfloat16),
        values,
        preferred_element_type=jnp.float32,
    )
    summed_values, summed_total = lax.psum((local_values, local_total), "seq")
    kernel_values = summed_values / summed_total[:, :, None]
    scores_a = (
        jnp.einsum(
            "buq,juq->ubj",
            query_landmark_rows,
            key_landmark_rows,
            preferred_element_type=jnp.float32,
        )
        * score_scale
    )
    landmark_kernel = softmax_last(scores_a)
    inverse = newton_inverse(landmark_kernel, NEWTON_STEPS)
    blended_value_rows = highest_product(inverse, kernel_values).astype(jnp.bfloat16)
    scores_f = (
        jnp.einsum("fxr,yxr->xfy", queries, key_landmark_rows, preferred_element_type=jnp.float32)
        * score_scale
    )
    query_weight_rows = softmax_last(scores_f).astype(jnp.bfloat16)
    attended = jnp.einsum(
        "gxz,gzq->xgq", query_weight_rows, blended_value_rows, preferred_element_type=jnp.float32
    )
    local_squares = jnp.sum(attended * attended, axis=(1, 2))
    total_squares = lax.psum(local_squares, "head")
    feature_count = attended.shape[1] * attended.shape[2] * lax.axis_size("head")
    factor = 1.0 / jnp.sqrt(total_squares / feature_count + epsilon)
    return (attended * factor[:, None, None] * output_gain[None]).astype(jnp.bfloat16)


def solution(mesh):
    return jax.shard_map(
        on_device,
        mesh=mesh,
        in_specs=(
            P("seq", "head", None),
            P("seq", "head", None),
            P("seq", "head", None),
            P("head", None),
        ),
        out_specs=P("seq", "head", None),
        check_vma=False,
    )
```

profile of v0, /device:TPU:0, one launch (start us, length us, event | category | flops | bytes accessed | tf_op | source)
XLA Modules:
  0.0 481.8 jit_solution(9435257844551767336)
XLA Ops:
  6.5 0.0 copy-start
  6.5 2.1 convert_reduce_fusion.1
  8.7 51.4 %all_gather.6 = bf16[512,2,128]{2,0,1:T(8,128)(2,1)S(1)} all-gather(bf16[8,2,128]{2,0,1:T(8,128)(2,1)S(1)} %fusion.55), channel_id=1, replica_groups=mesh['seq'=64,'head'=4] {'seq'}, dimensions={0}, use_global_device_ids=true | all-gather | bytes 266240 | tf_op jit(solution)/shard_map/all_gather | solution.py:54
  60.1 5.8 %multiply_reduce_fusion = (f32[2,512]{1,0:T(2,128)S(1)}, f32[2,512,2048]{2,1,0:T(8,128)}) fusion(bf16[512,2,128]{2,0,1:T(8,128)(2,1)S(1)} %all_gather.6, bf16[2048,2,128]{2,1,0:T(2,128)(2,1)} %param.5), kind=kOutput, calls=%fused_computation.8 | convolution fusion | flops 541064192 | bytes 9703424 | tf_op jit(solution)/shard_map/nio,zio->inz/dot_general | solution.py:58
  65.9 126.7 %pmax.7 = f32[2,512]{1,0:T(2,128)S(1)} all-reduce(f32[2,512]{1,0:T(2,128)S(1)} %get-tuple-element.9), channel_id=1, replica_groups=mesh['seq'=64,'head'=4] {'seq'}, use_global_device_ids=true, to_apply=%region_9.0 | all-reduce | flops 1024 | bytes 8192 | tf_op jit(solution)/shard_map/pmax | solution.py:67
  192.5 5.8 %fusion.9 = f32[2,512,128]{2,1,0:T(8,128)} fusion(f32[2,512,2048]{2,1,0:T(8,128)} %get-tuple-element.10, f32[2,512]{1,0:T(2,128)S(1)} %pmax.7, bf16[2048,2,128]{2,1,0:T(2,128)(2,1)S(1)} %copy-done), kind=kOutput, calls=%fused_computation.12 | convolution fusion | flops 543162368 | bytes 9965568 | tf_op jit(solution)/shard_map/jqo,ojw->jqw/dot_general | solution.py:70
  198.3 0.0 all-reduce.2.cloned.1.call-update
  198.4 0.8 convert_reduce_fusion
  199.2 46.8 %all_gather.7 = bf16[512,2,128]{2,0,1:T(8,128)(2,1)S(1)} all-gather(bf16[8,2,128]{2,0,1:T(8,128)(2,1)S(1)} %fusion.54), channel_id=1, replica_groups=mesh['seq'=64,'head'=4] {'seq'}, dimensions={0}, use_global_device_ids=true | all-gather | bytes 266240 | tf_op jit(solution)/shard_map/all_gather | solution.py:55
  246.0 1.8 fusion.64
  247.9 0.0 copy-start.10
  247.9 3.0 convolution_multiply_fusion
  250.8 1.1 fusion.41
  251.9 1.1 fusion.42
  253.0 1.1 fusion.43
  254.1 0.6 fusion.46
  254.7 0.1 reduce_max.46
  254.8 0.1 reduce_max.47
  255.0 1.8 bitcast_divide_fusion
  256.8 1.8 copy.26
  258.6 7.0 %online-softmax = f32[2,512,512]{2,1,0:T(8,128)} custom-call(f32[2,512,512]{2,1,0:T(8,128)} %convolution_multiply_fusion, f32[2,512,512]{2,1,0:T(8,128)} %copy.26), custom_call_target="tpu_custom_call" | custom-call | tf_op online-softmax
  265.6 6.3 %fusion.17 = f32[2,512,512]{2,1,0:T(8,128)S(1)} fusion(f32[2,512,512]{2,1,0:T(8,128)} %online-softmax, f32[512,512]{1,0:T(8,128)} %fusion.41), kind=kOutput, calls=%fused_computation.19 | convolution fusion | flops 3221749760 | bytes 5242880 | tf_op jit(solution)/shard_map/hij,hjk->hik/dot_general | solution.py:31
  271.9 0.0 copy-done.2
  271.9 0.0 copy-done.6
  271.9 0.0 copy-start.4
  271.9 3.6 fusion.26
  275.6 5.0 %fusion.24 = f32[2,512,512]{2,1,0:T(8,128)} fusion(f32[2,512,512]{2,1,0:T(8,128)S(1)} %fusion.26, f32[2,512,512]{1,2,0:T(8,128)S(1)} %bitcast_divide_fusion, f32[512,512]{1,0:T(8,128)S(1)} %copy-done.4), kind=kOutput, calls=%fused_computation.31 | convolution fusion | flops 3222274048 | bytes 7340032 | tf_op jit(solution)/shard_map/hij,hjk->hik/dot_general | solution.py:31
  280.6 7.0 %online-softmax.1 = f32[2,512,512]{2,1,0:T(8,128)} custom-call(f32[2,512,512]{2,1,0:T(8,128)} %convolution_multiply_fusion, f32[2,512,512]{2,1,0:T(8,128)} %fusion.24), custom_call_target="tpu_custom_call" | custom-call | tf_op online-softmax
  287.6 0.0 copy-done.3
  287.6 2.1 copy.28
  289.7 4.4 fusion.5
  294.1 0.0 copy-done.12
  294.1 0.0 copy-start.1
  294.1 0.0 copy-start.8
  294.1 4.5 fusion.30
  298.6 0.0 copy-done.1
  298.6 3.6 fusion.15
  302.2 0.0 copy-done.7
  302.2 3.6 fusion.21
  305.9 126.9 %psum.22 = f32[2,512]{1,0:T(2,128)S(1)} all-reduce(f32[2,512]{1,0:T(2,128)S(1)} %fusion.5), channel_id=1, replica_groups=mesh['seq'=64,'head'=4] {'seq'}, use_global_device_ids=true, to_apply=%region_12.0 | all-reduce | flops 1024 | bytes 8192 | tf_op jit(solution)/shard_map/psum | solution.py:76
  432.8 7.9 %fusion.65 = f32[2,2048]{1,0:T(2,128)S(1)} fusion(f32[2,512,2048]{2,1,0:T(8,128)} %fusion.30), kind=kOutput, calls=%fused_computation.75 | output fusion | flops 8389119 | bytes 8404992 | tf_op jit(solution)/shard_map/sub | solution.py:15
  440.8 5.1 %fusion.19 = f32[2,512,512]{2,1,0:T(8,128)} fusion(f32[2,512,512]{2,1,0:T(8,128)S(1)} %fusion.21, f32[2,512,512]{1,2,0:T(8,128)S(1)} %copy-done.9, f32[512,512]{1,0:T(8,128)S(1)} %copy-done.5), kind=kOutput, calls=%fused_computation.26 | convolution fusion | flops 3222274048 | bytes 7340032 | tf_op jit(solution)/shard_map/hij,hjk->hik/dot_general | solution.py:31
  445.8 3.7 convolution_convert_fusion
  449.5 0.0 copy-start.14
  449.5 10.3 %multiply_reduce_fusion.1 = (f32[2048]{0:T(1024)S(1)}, f32[2,128,2048]{2,1,0:T(8,128)}) fusion(bf16[2,512,128]{2,1,0:T(8,128)(2,1)S(1)} %convolution_convert_fusion, f32[2,2048]{1,0:T(2,128)S(1)} %fusion.65, f32[2,512,2048]{2,1,0:T(8,128)} %fusion.30), kind=kOutput, calls=%fused_computation.25 | convolution fusion | flops 548407808 | bytes 10772480 | tf_op jit(solution)/shard_map/gxz,gzq->xgq/dot_general | solution.py:95
  459.8 10.9 %psum.23 = f32[2048]{0:T(1024)S(1)} all-reduce(f32[2048]{0:T(1024)S(1)} %get-tuple-element.11), channel_id=1, replica_groups=mesh['seq'=64,'head'=4] {'head'}, use_global_device_ids=true, to_apply=%region_16.0 | all-reduce | flops 2048 | bytes 16384 | tf_op jit(solution)/shard_map/psum | solution.py:99
  470.7 1.8 fusion.29
  472.5 2.0 copy.35
  (24 shorter events, 0.1 us)
Async XLA Ops:
  6.5 186.0 %copy-start = (bf16[2048,2,128]{2,1,0:T(2,128)(2,1)S(1)}, bf16[2048,2,128]{2,1,0:T(2,128)(2,1)}, u32[]{:S(2)}) copy-start(bf16[2048,2,128]{2,1,0:T(2,128)(2,1)} %param.6) | copy-start | bytes 3145732
  6.5 439.3 %all-reduce.2.cloned.1.call-start = ((), (), s32[]{:S(2)}) async-start(), calls=%async_computation | async-start | bytes 1048576 | tf_op jit(solution)/shard_map/psum | solution.py:76
  60.1 5.8 %copy-start.13 = (bf16[512,2,128]{2,0,1:T(8,128)(2,1)}, bf16[512,2,128]{2,0,1:T(8,128)(2,1)S(1)}, u32[]{:S(2)}) copy-start(bf16[512,2,128]{2,0,1:T(8,128)(2,1)S(1)} %all_gather.6) | copy-start | bytes 786436
  192.5 5.8 %copy-start.11 = (bf16[2048,2,128]{2,1,0:T(2,128)(2,1)S(1)}, bf16[2048,2,128]{2,1,0:T(2,128)(2,1)}, u32[]{:S(2)}) copy-start(bf16[2048,2,128]{2,1,0:T(2,128)(2,1)} %param.5) | copy-start | bytes 3145732
  247.9 6.3 %copy-start.10 = (f32[2,512,512]{2,1,0:T(8,128)}, f32[2,512,512]{2,1,0:T(8,128)S(1)}, u32[]{:S(2)}) copy-start(f32[2,512,512]{2,1,0:T(8,128)S(1)} %get-tuple-element.8) | copy-start | bytes 6291460
  265.6 6.3 %copy-start.2 = (f32[2,512,512]{2,1,0:T(8,128)S(1)}, f32[2,512,512]{2,1,0:T(8,128)}, u32[]{:S(2)}) copy-start(f32[2,512,512]{2,1,0:T(8,128)} %online-softmax) | copy-start | bytes 6291460
  265.6 6.3 %copy-start.6 = (f32[512,512]{1,0:T(8,128)S(1)}, f32[512,512]{1,0:T(8,128)}, u32[]{:S(2)}) copy-start(f32[512,512]{1,0:T(8,128)} %fusion.42) | copy-start | bytes 3145732
  271.9 3.7 copy-start.4
  280.6 7.0 %copy-start.3 = (f32[2,512,512]{2,1,0:T(8,128)S(1)}, f32[2,512,512]{2,1,0:T(8,128)}, u32[]{:S(2)}) copy-start(f32[2,512,512]{2,1,0:T(8,128)} %fusion.24) | copy-start | bytes 6291460
  289.7 4.4 copy-start.12
  294.1 4.5 copy-start.1
  294.1 4.5 copy-start.8
  298.6 3.7 copy-start.7
  432.8 8.0 %copy-start.5 = (f32[512,512]{1,0:T(8,128)S(1)}, f32[512,512]{1,0:T(8,128)}, u32[]{:S(2)}) copy-start(f32[512,512]{1,0:T(8,128)} %fusion.43) | copy-start | bytes 3145732
  432.8 8.0 %copy-start.9 = (f32[2,512,512]{1,2,0:T(8,128)S(1)}, f32[2,512,512]{1,2,0:T(8,128)}, u32[]{:S(2)}) copy-start(f32[2,512,512]{1,2,0:T(8,128)} %copy.28) | copy-start | bytes 6291460
  449.5 21.2 %copy-start.14 = (f32[2,128]{1,0:T(2,128)S(1)}, f32[2,128]{1,0:T(2,128)}, u32[]{:S(2)}) copy-start(f32[2,128]{1,0:T(2,128)} %param.7) | copy-start | bytes 3076
Sparse Core Ops, SparseCore 0:
  198.5 179.0 all-reduce.1
where the time goes:
time: 490 us; the launch traced here: 482 us
  blocking collectives  363 us (74%)
  matrix products  62.1 us (13%)
  other arithmetic  23 us (5%)
  between operations  14.1 us (3%)
  Pallas kernels  14 us (3%)
  local copies, waits for them, and re-layouts  5.95 us (1%)
    psum x1, blocking collectives, on_device(): summed_values, summed_total = lax.psum((local_values, local_total), 'seq')  127 us
    pmax x1, blocking collectives, on_device(): row_top = lax.pmax(local_top, 'seq')  127 us
    all_gather x1, blocking collectives, on_device(): lax.all_gather(query_marks, 'seq', axis=0, tiled=True)  51.4 us
    all_gather x1, blocking collectives, on_device(): lax.all_gather(key_marks, 'seq', axis=0, tiled=True)  46.8 us
    dot_general x7, matrix products, highest_product(): jnp.einsum('hij,hjk->hik', first_factor, second_factor, precision=lax.Pre...  30.9 us
    unnamed x2, Pallas kernels  14 us
    psum x1, blocking collectives, on_device(): total_squares = lax.psum(local_squares, 'head')  10.9 us
    dot_general x1, matrix products, on_device(): jnp.einsum('gxz,gzq->xgq', query_weight_rows, blended_value_rows, preferr...  10.3 us
  transfers between devices with their start and end apart: 1, of which 0 were waited for; matrix products, arithmetic and copies ran while one was open for 12% of the time, Pallas kernels for 3%

commit v1 on v0

v1 whole, which is shorter than its diff:
```python
import functools

import jax
import jax.numpy as jnp
from jax import lax
from jax.experimental import pallas as pl
from jax.experimental.pallas import tpu as pltpu
from jax.sharding import PartitionSpec as P

MESH = pl.DeviceIdType.MESH
F32 = jnp.float32
BF16 = jnp.bfloat16
NZ, NX, NC, NY = 8, 4, 2, 4
TOKENS = 2048
DIM = 128
MARKS = 512
SEGMENT = 256
EPSILON = 1e-06
LOG2E = 1.4426950408889634
SCALE2 = DIM ** (-0.5) * LOG2E

NN = (((1,), (0,)), ((), ()))
NT = (((1,), (1,)), ((), ()))


def dot(a, b, dims=NN):
    return lax.dot_general(a, b, dims, preferred_element_type=F32)


def split(a):
    high = a.astype(BF16)
    return high, (a - high.astype(F32)).astype(BF16)


def dot3(a, b, dims=NN):
    return dot(a[0], b[0], dims) + (dot(a[0], b[1], dims) + dot(a[1], b[0], dims))


def merge(values, tops):
    top = functools.reduce(jnp.maximum, tops)
    weights = [jnp.exp2(t - top) for t in tops]
    total = functools.reduce(jnp.add, weights)
    scale = 1.0 / total
    merged = functools.reduce(jnp.add, [v * (w * scale) for v, w in zip(values, weights)])
    return merged, top + jnp.log2(total)


def kernel(
    q_hbm, k_hbm, v_hbm, gain_ref, o_hbm,
    xq, xk, xv, qh, kh, vt, marks, gq, gk, mq, mk, wide,
    mine, away, rcore, xsum, rx, zsum, rz, kvt, kvf, weights_f,
    a_ref, t0, t1, t2, w_ref, mixt, att, sqs, sqr, out,
    local_sem, ssem, rsem,
):
    s = lax.axis_index("seq")
    y = lax.axis_index("head")
    c = lax.rem(s, 2)
    x = lax.rem(lax.div(s, 2), NX)
    z = lax.div(s, 2 * NX)
    other = 1 - c

    def at_z(d):
        zz = lax.rem(z + d, NZ)
        return {"seq": (zz * NX + x) * 2 + c}

    def at_x(d):
        xx = lax.rem(x + d, NX)
        return {"seq": (z * NX + xx) * 2 + c}

    sibling = {"seq": (z * NX + x) * 2 + other}

    def at_y(d):
        return {"head": lax.rem(y + d, NY)}

    counter = [0]
    started = []

    def send(src, dst, target):
        n = counter[0]
        counter[0] += 1
        copy = pltpu.make_async_remote_copy(
            src_ref=src, dst_ref=dst, send_sem=ssem.at[n], recv_sem=rsem.at[n],
            device_id=target, device_id_type=MESH,
        )
        copy.start()
        started.append(copy)
        return copy

    loads = [
        pltpu.make_async_copy(src, dst, local_sem.at[i])
        for i, (src, dst) in enumerate(((q_hbm, xq), (k_hbm, xk), (v_hbm, xv)))
    ]
    for load in loads:
        load.start()

    barrier = pltpu.get_barrier_semaphore()
    peers = [at_z(d) for d in range(1, NZ)] + [at_x(d) for d in range(1, NX)] + [sibling]
    peers += [at_y(d) for d in range(1, NY)]
    for peer in peers:
        pl.semaphore_signal(barrier, inc=1, device_id=peer, device_id_type=MESH)

    def means(src, dst):
        for j in range(TOKENS // SEGMENT):
            rows = src[pl.ds(j * 2 * SEGMENT, 2 * SEGMENT), :].astype(F32)
            total = jnp.sum(rows.reshape(2 * SEGMENT // 8, 8, DIM), axis=0)
            total = total + pltpu.roll(total, 4, 0)
            total = total + pltpu.roll(total, 2, 0)
            marks[j : j + 1, :] = total[0:1]
            marks[8 + j : 9 + j, :] = total[1:2]
        dst[c, x, z] = (marks[...] * (1.0 / SEGMENT)).astype(BF16)

    def gather_z(g):
        return [send(g.at[c, x, z], g.at[c, x, z], at_z(d)) for d in range(1, NZ)]

    def gather_x(g):
        return [send(g.at[c, x], g.at[c, x], at_x(d)) for d in range(1, NX)]

    def gather_core(g):
        return [send(g.at[c], g.at[c], sibling)]

    def arrived(copies):
        for copy in copies:
            copy.wait_recv()

    def head_rows(src, visit):
        def body(j, _):
            wide[...] = src[pl.ds(j * 512, 512), :].astype(F32)
            for h in range(2):
                visit(h, j, wide[pl.ds(h, 256, stride=2), :].astype(BF16))
            return 0

        lax.fori_loop(0, TOKENS // 256, body, 0)

    eye = (
        lax.broadcasted_iota(jnp.int32, (DIM, DIM), 0) == lax.broadcasted_iota(jnp.int32, (DIM, DIM), 1)
    ).astype(BF16)

    def keep_q(h, j, rows):
        qh[h, pl.ds(j * 256, 256), :] = rows

    def keep_k(h, j, rows):
        kh[h, pl.ds(j * 256, 256), :] = rows

    def keep_v(h, j, rows):
        vt[h, j] = dot(eye, rows, NT).astype(BF16)

    loads[0].wait()
    means(xq, gq)
    pl.semaphore_wait(barrier, len(peers))
    q_copies = gather_z(gq)
    loads[1].wait()
    means(xk, gk)
    k_copies = gather_z(gk)
    head_rows(xk, keep_k)
    arrived(q_copies)
    q_copies = gather_x(gq)
    arrived(k_copies)
    k_copies = gather_x(gk)
    loads[2].wait()
    head_rows(xv, keep_v)
    arrived(q_copies)
    q_copies = gather_core(gq)
    arrived(k_copies)
    k_copies = gather_core(gk)
    head_rows(xq, keep_q)
    arrived(q_copies)

    def landmarks(g, m):
        rows = g[...].astype(F32).reshape(NC * NX * NZ, 16, DIM)
        for h in range(2):
            m[h] = rows[:, 8 * h : 8 * h + 8, :].reshape(MARKS, DIM).astype(BF16)

    landmarks(gq, mq)

    def local_part(h, half, dst):
        scores = dot(kh[h], mq[h, pl.ds(half * 256, 256), :], NT)
        top = jnp.max(scores, axis=0, keepdims=True)
        weights = jnp.exp2((scores - top) * SCALE2)
        total = jnp.sum(weights, axis=0, keepdims=True)
        weights = weights.astype(BF16)
        part = dot(vt[h, 0], weights[0:256])
        for j in range(1, TOKENS // 256):
            part = part + dot(vt[h, j], weights[256 * j : 256 * j + 256])
        part = part * (1.0 / total)
        log_sum = top * SCALE2 + jnp.log2(total)
        for i in range(2):
            cut = slice(128 * i, 128 * i + 128)
            dst[2 * half + i, 0:DIM, :] = part[:, cut]
            dst[2 * half + i, DIM : DIM + 8, :] = jnp.broadcast_to(log_sum[:, cut], (8, 128))

    core_copies = []
    for half in range(2):
        local_part(other, half, away)
        cut = pl.ds(2 * half, 2)
        core_copies.append(send(away.at[cut], rcore.at[cut], sibling))
    for half in range(2):
        local_part(c, half, mine)

    for half in range(2):
        core_copies[half].wait_recv()
        for i in (2 * half, 2 * half + 1):
            value, log_sum = merge(
                [mine[i, 0:DIM, :], rcore[i, 0:DIM, :]],
                [mine[i, DIM : DIM + 1, :], rcore[i, DIM : DIM + 1, :]],
            )
            xsum[i, 0:DIM, :] = value
            xsum[i, DIM : DIM + 8, :] = jnp.broadcast_to(log_sum, (8, 128))
    x_copies = [send(xsum.at[lax.rem(x + d, NX)], rx.at[d - 1], at_x(d)) for d in range(1, NX)]

    arrived(k_copies)
    landmarks(gk, mk)
    scores = dot(mq[c], mk[c], NT)
    weights = jnp.exp2((scores - jnp.max(scores, axis=1, keepdims=True)) * SCALE2)
    a = weights * (1.0 / jnp.sum(weights, axis=1, keepdims=True))
    magnitude = jnp.abs(a)
    column_top = jnp.max(jnp.sum(magnitude, axis=0, keepdims=True), axis=1, keepdims=True)
    row_top = jnp.max(jnp.sum(magnitude, axis=1, keepdims=True), axis=0, keepdims=True)
    shrink = 1.0 / (column_top * row_top)
    a_ref[...] = a

    def eye_times(f):
        i = lax.broadcasted_iota(jnp.int32, (MARKS, MARKS), 0)
        j = lax.broadcasted_iota(jnp.int32, (MARKS, MARKS), 1)
        return jnp.where(i == j, F32(f), F32(0.0))

    a2 = split(a)
    t0[...] = dot3(a2, a2, NT) * shrink
    p0 = split(t0[...])
    t1[...] = dot3(p0, p0)

    arrived(x_copies)
    blocks = [xsum[x]] + [rx[d] for d in range(NX - 1)]
    value, log_sum = merge([b[0:DIM] for b in blocks], [b[DIM : DIM + 1] for b in blocks])
    log_sum = jnp.broadcast_to(log_sum, (8, 128))
    for i in range(NZ):
        zsum[i, 0:16, :] = value[16 * i : 16 * i + 16]
        zsum[i, 16:24, :] = log_sum
    z_copies = [send(zsum.at[lax.rem(z + d, NZ)], rz.at[d - 1], at_z(d)) for d in range(1, NZ)]

    s2 = split(t1[...])
    t2[...] = dot3(s2, p0)
    w_ref[...] = eye_times(13.0) - 15.0 * t0[...] + 7.0 * t1[...] - t2[...]
    t2[...] = 0.25 * dot3(p0, split(w_ref[...]))

    arrived(z_copies)
    blocks = [zsum[z]] + [rz[d] for d in range(NZ - 1)]
    value, _ = merge([b[0:16] for b in blocks], [b[16:17] for b in blocks])
    kvt[x, pl.ds(pl.multiple_of(16 * z, 16), 16), :] = value
    piece = kvt.at[x, pl.ds(pl.multiple_of(16 * z, 16), 16)]
    kv_copies = [send(piece, piece, at_z(d)) for d in range(1, NZ)]

    p1 = split(t2[...])
    t0[...] = dot3(p1, p1)
    t1[...] = eye_times(13.0) - 15.0 * t2[...] + dot3(split(t0[...]), split(eye_times(7.0) - t2[...]))

    arrived(kv_copies)
    kv_copies = [send(kvt.at[x], kvt.at[x], at_x(d)) for d in range(1, NX)]

    w_ref[...] = dot3(split(w_ref[...]), split(t1[...])) * (shrink * 0.0625)

    def query_weights(n, _):
        h = lax.div(n, TOKENS // 256)
        rows = pl.ds(pl.multiple_of(lax.rem(n, TOKENS // 256) * 256, 256), 256)
        scores = dot(qh[h, rows, :], mk[h], NT)
        weights = jnp.exp2((scores - jnp.max(scores, axis=1, keepdims=True)) * SCALE2)
        weights = weights * (1.0 / jnp.sum(weights, axis=1, keepdims=True))
        weights_f[h, rows, :] = weights.astype(BF16)
        return 0

    lax.fori_loop(0, 2 * TOKENS // 256, query_weights, 0)

    arrived(kv_copies)
    for i in range(NX):
        kvf[:, 128 * i : 128 * i + 128] = kvt[i]
    blended = dot3(split(kvf[...]), split(w_ref[...]))
    mixt[c] = dot3(split(blended), split(a_ref[...])).astype(BF16)
    mix_copy = send(mixt.at[c], mixt.at[c], sibling)

    def attend(h):
        def body(n, _):
            rows = pl.ds(pl.multiple_of(n * 256, 256), 256)
            att[h, rows, :] = dot(weights_f[h, rows, :], mixt[h], NT)
            return 0

        lax.fori_loop(0, TOKENS // 256, body, 0)

    attend(c)
    mix_copy.wait_recv()
    attend(other)

    ones = jnp.ones((8, DIM), BF16)
    for n in range(TOKENS // 256):
        rows = pl.ds(n * 256, 256)
        first, second = att[0, rows, :], att[1, rows, :]
        high, low = split(first * first + second * second)
        squares = dot(ones, high, NT) + dot(ones, low, NT)
        for i in range(2):
            sqs[2 * n + i : 2 * n + i + 1, :] = squares[0:1, 128 * i : 128 * i + 128]
    y_copies = [send(sqs, sqr.at[d - 1], at_y(d)) for d in range(1, NY)]
    arrived(y_copies)
    total = sqs[...] + sqr[0] + sqr[1] + sqr[2]
    sqs_factor = lax.rsqrt(total * (1.0 / (8 * DIM)) + EPSILON)

    stores = []
    for n in range(TOKENS // 128):
        rows = pl.ds(n * 128, 128)
        factor = jnp.broadcast_to(sqs_factor[n : n + 1, :], (DIM, DIM)).T
        for h in range(2):
            wide[pl.ds(h, 128, stride=2), :] = att[h, rows, :] * factor * gain_ref[h : h + 1, :]
        out[pl.ds(n * 256, 256), :] = wide[0:256, :].astype(BF16)
        if n % 4 == 3:
            cut = pl.ds((n - 3) * 256, 1024)
            store = pltpu.make_async_copy(out.at[cut], o_hbm.at[cut], local_sem.at[3 + n // 4])
            store.start()
            stores.append(store)
    for copy in started:
        copy.wait_send()
    for store in stores:
        store.wait()


def on_device(queries, key_rows, values, gain):
    rows = 2 * TOKENS
    args = [a.reshape(rows, DIM) for a in (queries, key_rows, values)]
    vmem = pltpu.VMEM
    out = pl.pallas_call(
        kernel,
        out_shape=jax.ShapeDtypeStruct((rows, DIM), BF16),
        in_specs=[pl.BlockSpec(memory_space=pl.ANY)] * 3 + [pl.BlockSpec(memory_space=pltpu.VMEM)],
        out_specs=pl.BlockSpec(memory_space=pl.ANY),
        scratch_shapes=[
            vmem((rows, DIM), BF16),
            vmem((rows, DIM), BF16),
            vmem((rows, DIM), BF16),
            vmem((2, TOKENS, DIM), BF16),
            vmem((2, TOKENS, DIM), BF16),
            vmem((2, TOKENS // 256, DIM, 256), BF16),
            vmem((16, DIM), F32),
            vmem((NC, NX, NZ, 16, DIM), BF16),
            vmem((NC, NX, NZ, 16, DIM), BF16),
            vmem((2, MARKS, DIM), BF16),
            vmem((2, MARKS, DIM), BF16),
            vmem((512, DIM), F32),
            vmem((NX, DIM + 8, DIM), F32),
            vmem((NX, DIM + 8, DIM), F32),
            vmem((NX, DIM + 8, DIM), F32),
            vmem((NX, DIM + 8, DIM), F32),
            vmem((NX - 1, DIM + 8, DIM), F32),
            vmem((NZ, 24, DIM), F32),
            vmem((NZ - 1, 24, DIM), F32),
            vmem((NX, DIM, DIM), F32),
            vmem((DIM, MARKS), F32),
            vmem((2, TOKENS, MARKS), BF16),
            vmem((MARKS, MARKS), F32),
            vmem((MARKS, MARKS), F32),
            vmem((MARKS, MARKS), F32),
            vmem((MARKS, MARKS), F32),
            vmem((MARKS, MARKS), F32),
            vmem((2, DIM, MARKS), BF16),
            vmem((2, TOKENS, DIM), F32),
            vmem((16, DIM), F32),
            vmem((NY - 1, 16, DIM), F32),
            vmem((rows, DIM), BF16),
            pltpu.SemaphoreType.DMA((8,)),
            pltpu.SemaphoreType.DMA((48,)),
            pltpu.SemaphoreType.DMA((48,)),
        ],
        compiler_params=pltpu.CompilerParams(
            collective_id=0, has_side_effects=True, vmem_limit_bytes=56 * 1024 * 1024
        ),
    )(*args, gain)
    return out.reshape(TOKENS, 2, DIM)


def solution(mesh):
    spec = P("seq", "head", None)
    return jax.shard_map(
        on_device,
        mesh=mesh,
        in_specs=(spec, spec, spec, P("head", None)),
        out_specs=spec,
        check_vma=False,
    )
```

time: 490 us -> 63.1 us (0.13)
  the two profiles are of different devices: /device:TPU:0 before, /device:TPU:1 now
where the time goes in v1:
time: 63.1 us; the launch traced here: 63 us
  Pallas kernels  60.4 us (96%)
  local copies, waits for them, and re-layouts  2.58 us (4%)
    pallas_call x1, Pallas kernels, on_device(): pl.pallas_call(kernel, out_shape=jax.ShapeDtypeStruct((rows, DIM), BF16),...  60.4 us
    unnamed x1, local copies, waits for them, and re-layouts  2.58 us

profile of v1, /device:TPU:1, one launch (start us, length us, event | category | flops | bytes accessed | tf_op | source)
XLA Modules:
  0.0 63.0 jit_solution(17682994007599434054)
XLA Ops:
  0.0 60.4 %shard_map.46 = bf16[4096,128]{1,0:T(8,128)(2,1)} custom-call(bf16[4096,128]{1,0:T(8,128)(2,1)} %bitcast.5, bf16[4096,128]{1,0:T(8,128)(2,1)} %bitcast.6, bf16[4096,128]{1,0:T(8,128)(2,1)} %bitcast.7, f32[2,128]{1,0:T(2,128)} %gain_ref.1), custom_call_target="tpu_custom_call" | custom-call | tf_op jit(solution)/shard_map/pallas_call | solution.py:326
  60.4 2.6 %copy.6 = bf16[2048,2,128]{2,1,0:T(2,128)(2,1)} copy(bf16[2048,2,128]{2,1,0:T(2,128)(2,1)} %bitcast.4) | data formatting | bytes 2097152

commit v2 on v1

v2 whole, which is shorter than its diff:
```python
import jax
import jax.numpy as jnp
from jax import lax
from jax.experimental import pallas as pl
from jax.experimental.pallas import tpu as pltpu
from jax.sharding import PartitionSpec as P

MESH = pl.DeviceIdType.MESH
F32 = jnp.float32
BF16 = jnp.bfloat16
NZ, NX, NC, NY = 8, 4, 2, 4
TOKENS = 2048
DIM = 128
MARKS = 512
SEGMENT = 256
EPSILON = 1e-06
LOG2E = 1.4426950408889634
SCALE2 = DIM ** (-0.5) * LOG2E

NN = (((1,), (0,)), ((), ()))
NT = (((1,), (1,)), ((), ()))


def dot(a, b, dims=NN):
    return lax.dot_general(a, b, dims, preferred_element_type=F32)


def split(a):
    high = a.astype(BF16)
    return high, (a - high.astype(F32)).astype(BF16)


def dot3(a, b, dims=NN):
    return dot(a[0], b[0], dims) + (dot(a[0], b[1], dims) + dot(a[1], b[0], dims))


PEERS = sorted(
    ((dz, dx) for dz in range(NZ) for dx in range(NX) if dz or dx),
    key=lambda p: -(min(p[0], NZ - p[0]) + min(p[1], NX - p[1])),
)
NP = len(PEERS)


def kernel(
    q_hbm, k_hbm, v_hbm, gain_ref, o_hbm,
    xq, xk, xv, qh, kh, vh, marks, gq, gk, mq, mk, wide,
    away, rcore, parts, logs, rparts, rlogs, kvt, kvf, weights_f, totals,
    t0, t1, t2, w_ref, mixt, attt, att, sqs, sqr, out,
    local_sem, ssem, rsem,
):
    s = lax.axis_index("seq")
    y = lax.axis_index("head")
    c = lax.rem(s, 2)
    x = lax.rem(lax.div(s, 2), NX)
    z = lax.div(s, 2 * NX)
    other = 1 - c

    def at(d):
        return lax.rem(z + d[0], NZ), lax.rem(x + d[1], NX)

    def chip(d):
        zz, xx = at(d)
        return {"seq": (zz * NX + xx) * 2 + c}

    sibling = {"seq": (z * NX + x) * 2 + other}

    def at_y(d):
        return {"head": lax.rem(y + d, NY)}

    started = []

    def remote(src, dst, target, n):
        return pltpu.make_async_remote_copy(
            src_ref=src, dst_ref=dst, send_sem=ssem.at[n], recv_sem=rsem.at[n],
            device_id=target, device_id_type=MESH,
        )

    def send(src, dst, target):
        copy = remote(src, dst, target, len(started))
        copy.start()
        started.append(copy)
        return copy

    def send_all(pieces, size_of):
        n = len(started)
        for src, dst, d in pieces:
            remote(src, dst, chip(d), n).start()
        started.append(remote(size_of, size_of, sibling, n))
        return started[n]

    def arrived(copies):
        for copy in copies:
            copy.wait_recv()

    loads = [
        pltpu.make_async_copy(src, dst, local_sem.at[i])
        for i, (src, dst) in enumerate(((q_hbm, xq), (k_hbm, xk), (v_hbm, xv)))
    ]
    for load in loads:
        load.start()

    barrier = pltpu.get_barrier_semaphore()
    peers = [chip(d) for d in PEERS] + [sibling] + [at_y(d) for d in range(1, NY)]
    for peer in peers:
        pl.semaphore_signal(barrier, inc=1, device_id=peer, device_id_type=MESH)

    def means(src, dst):
        for j in range(TOKENS // SEGMENT):
            rows = src[pl.ds(j * 2 * SEGMENT, 2 * SEGMENT), :].astype(F32)
            total = jnp.sum(rows.reshape(2 * SEGMENT // 8, 8, DIM), axis=0)
            total = total + pltpu.roll(total, 4, 0)
            total = total + pltpu.roll(total, 2, 0)
            marks[j : j + 1, :] = total[0:1]
            marks[8 + j : 9 + j, :] = total[1:2]
        dst[c, x, z] = (marks[...] * (1.0 / SEGMENT)).astype(BF16)

    def spread(block):
        return [send_all([(block, block, d) for d in PEERS], rparts)]

    def head_rows(src, dst):
        def body(j, _):
            wide[0:512, :] = src[pl.ds(j * 512, 512), :].astype(F32)
            for h in range(2):
                dst[h, pl.ds(j * 256, 256), :] = wide[pl.ds(h, 256, stride=2), :].astype(BF16)
            return 0

        lax.fori_loop(0, TOKENS // 256, body, 0)

    def landmarks(g, m, core):
        rows = g[core].astype(F32).reshape(NX * NZ, 16, DIM)
        for h in range(2):
            m[h, core] = rows[:, 8 * h : 8 * h + 8, :].reshape(MARKS // 2, DIM).astype(BF16)

    loads[0].wait()
    means(xq, gq)
    pl.semaphore_wait(barrier, len(peers))
    q_copies = spread(gq.at[c, x, z])
    loads[1].wait()
    means(xk, gk)
    k_copies = spread(gk.at[c, x, z])
    head_rows(xk, kh)
    loads[2].wait()
    head_rows(xv, vh)
    head_rows(xq, qh)
    arrived(q_copies)
    q_copies = [send(gq.at[c], gq.at[c], sibling)]
    landmarks(gq, mq, c)

    def local_part(h, rows):
        scores = dot(rows, kh[h], NT)
        top = jnp.max(scores, axis=1, keepdims=True)
        weights = jnp.exp2((scores - top) * SCALE2)
        total = jnp.sum(weights, axis=1, keepdims=True)
        part = dot(weights.astype(BF16), vh[h]) * (1.0 / total)
        return part, jnp.broadcast_to(top * SCALE2 + jnp.log2(total), part.shape)

    core_copies = []

    def part_away(half):
        away[half, 0], away[half, 1] = local_part(other, mq[other, half])
        core_copies.append(send(away.at[half], rcore.at[half], sibling))

    part_away(c)
    arrived(q_copies)
    landmarks(gq, mq, other)
    part_away(other)
    arrived(k_copies)
    k_copies = [send(gk.at[c], gk.at[c], sibling)]
    value, log_sum = local_part(c, mq[c].reshape(MARKS, DIM))
    arrived(core_copies)
    far = jnp.concatenate([rcore[0, 0], rcore[1, 0]], axis=0)
    far_log = jnp.concatenate([rcore[0, 1], rcore[1, 1]], axis=0)
    top = jnp.maximum(log_sum, far_log)
    near_weight, far_weight = jnp.exp2(log_sum - top), jnp.exp2(far_log - top)
    total = near_weight + far_weight
    value = (value * near_weight + far * far_weight) * (1.0 / total)
    log_sum = top + jnp.log2(total)
    for i in range(NX):
        cut = slice(128 * i, 128 * i + 128)
        parts[i] = value[cut].T.astype(BF16).reshape(NZ, 16, DIM)
        logs[i] = log_sum[cut].T[0:1]
    log_pieces = [(logs.at[at(d)[1]], rlogs.at[n], d) for n, d in enumerate(PEERS)]
    part_pieces = [(parts.at[at(d)[1], at(d)[0]], rparts.at[n], d) for n, d in enumerate(PEERS)]
    reduce_copies = [send_all(log_pieces, rlogs), send_all(part_pieces, rparts)]

    arrived(k_copies)
    for core in range(2):
        landmarks(gk, mk, core)
    scores = dot(mq[c].reshape(MARKS, DIM), mk[c].reshape(MARKS, DIM), NT)
    weights = jnp.exp2((scores - jnp.max(scores, axis=1, keepdims=True)) * SCALE2)
    a = weights * (1.0 / jnp.sum(weights, axis=1, keepdims=True))
    magnitude = jnp.abs(a)
    column_top = jnp.max(jnp.sum(magnitude, axis=0, keepdims=True), axis=1, keepdims=True)
    row_top = jnp.max(jnp.sum(magnitude, axis=1, keepdims=True), axis=0, keepdims=True)
    shrink = 1.0 / (column_top * row_top)

    def eye_times(f):
        i = lax.broadcasted_iota(jnp.int32, (MARKS, MARKS), 0)
        j = lax.broadcasted_iota(jnp.int32, (MARKS, MARKS), 1)
        return jnp.where(i == j, F32(f), F32(0.0))

    a2 = split(a)
    t0[...] = dot3(a2, a2, NT) * shrink
    p0 = split(t0[...])
    t1[...] = dot3(p0, p0)
    s2 = split(t1[...])
    t2[...] = dot3(s2, p0)
    w_ref[...] = eye_times(13.0) - 15.0 * t0[...] + 7.0 * t1[...] - t2[...]
    t2[...] = 0.25 * dot3(p0, split(w_ref[...]))
    p1 = split(t2[...])
    t0[...] = dot3(p1, p1)

    arrived(reduce_copies)
    own_log, far_logs = logs[x], rlogs[...]
    top = jnp.maximum(own_log, jnp.max(far_logs, axis=0))
    own_weight, far_weights = jnp.exp2(own_log - top), jnp.exp2(far_logs - top[None])
    total = own_weight + jnp.sum(far_weights, axis=0)
    value = parts[x, z].astype(F32) * own_weight + jnp.sum(rparts[...].astype(F32) * far_weights, axis=0)
    kvt[x, z] = (value * (1.0 / total)).astype(BF16)
    kv_copies = spread(kvt.at[x, z])

    t1[...] = eye_times(13.0) - 15.0 * t2[...] + dot3(split(t0[...]), split(eye_times(7.0) - t2[...]))
    w_ref[...] = dot3(split(w_ref[...]), split(t1[...])) * (shrink * 0.0625)

    def query_weights(h, _):
        scores = dot(mk[h].reshape(MARKS, DIM), qh[h], NT)
        weights = jnp.exp2((scores - jnp.max(scores, axis=0, keepdims=True)) * SCALE2)
        totals[h] = jnp.sum(weights, axis=0, keepdims=True)
        weights_f[h] = weights.astype(BF16)
        return 0

    lax.fori_loop(0, 2, query_weights, 0)

    arrived(kv_copies)
    for i in range(NX):
        kvf[:, 128 * i : 128 * i + 128] = kvt[i].reshape(DIM, DIM)
    w2 = split(w_ref[...])
    blended = dot(kvf[...], w2[0]) + dot(kvf[...], w2[1])
    mixt[c] = dot3(split(blended), a2).astype(BF16)
    mix_copy = send(mixt.at[c], mixt.at[c], sibling)

    def attend(h):
        value = dot(mixt[h], weights_f[h]) * (1.0 / totals[h])
        attt[h] = value
        return jnp.sum(value * value, axis=0, keepdims=True)

    squares = attend(c)
    arrived([mix_copy])
    squares = squares + attend(other)
    for n in range(TOKENS // 128):
        sqs[n : n + 1, :] = squares[:, 128 * n : 128 * n + 128]
    y_copies = [send(sqs, sqr.at[d - 1], at_y(d)) for d in (2, 1, 3)]
    for n in range(TOKENS // 128):
        for h in range(2):
            att[h, pl.ds(n * 128, 128), :] = attt[h, :, 128 * n : 128 * n + 128].T * gain_ref[h : h + 1, :]
    arrived(y_copies)
    total = sqs[...] + sqr[0] + sqr[1] + sqr[2]
    factors = lax.rsqrt(total * (1.0 / (8 * DIM)) + EPSILON)

    stores = []
    for n in range(TOKENS // 128):
        rows = pl.ds(n * 128, 128)
        factor = jnp.broadcast_to(factors[n : n + 1, :], (DIM, DIM)).T
        for h in range(2):
            wide[pl.ds(n * 256 + h, 128, stride=2), :] = att[h, rows, :] * factor
        cut = pl.ds(n * 256, 256)
        out[cut, :] = wide[cut, :].astype(BF16)
        if n % 4 == 3:
            cut = pl.ds((n - 3) * 256, 1024)
            store = pltpu.make_async_copy(out.at[cut], o_hbm.at[cut], local_sem.at[3 + n // 4])
            store.start()
            stores.append(store)
    for copy in started:
        copy.wait_send()
    for store in stores:
        store.wait()


def on_device(queries, key_rows, values, gain):
    rows = 2 * TOKENS
    args = [a.reshape(rows, DIM) for a in (queries, key_rows, values)]
    vmem = pltpu.VMEM
    out = pl.pallas_call(
        kernel,
        out_shape=jax.ShapeDtypeStruct((rows, DIM), BF16),
        in_specs=[pl.BlockSpec(memory_space=pl.ANY)] * 3 + [pl.BlockSpec(memory_space=pltpu.VMEM)],
        out_specs=pl.BlockSpec(memory_space=pl.ANY),
        scratch_shapes=[
            vmem((rows, DIM), BF16),
            vmem((rows, DIM), BF16),
            vmem((rows, DIM), BF16),
            vmem((2, TOKENS, DIM), BF16),
            vmem((2, TOKENS, DIM), BF16),
            vmem((2, TOKENS, DIM), BF16),
            vmem((16, DIM), F32),
            vmem((NC, NX, NZ, 16, DIM), BF16),
            vmem((NC, NX, NZ, 16, DIM), BF16),
            vmem((2, 2, MARKS // 2, DIM), BF16),
            vmem((2, 2, MARKS // 2, DIM), BF16),
            vmem((rows, DIM), F32),
            vmem((2, 2, MARKS // 2, DIM), F32),
            vmem((2, 2, MARKS // 2, DIM), F32),
            vmem((NX, NZ, 16, DIM), BF16),
            vmem((NX, 1, DIM), F32),
            vmem((NP, 16, DIM), BF16),
            vmem((NP, 1, DIM), F32),
            vmem((NX, NZ, 16, DIM), BF16),
            vmem((DIM, MARKS), BF16),
            vmem((2, MARKS, TOKENS), BF16),
            vmem((2, 1, TOKENS), F32),
            vmem((MARKS, MARKS), F32),
            vmem((MARKS, MARKS), F32),
            vmem((MARKS, MARKS), F32),
            vmem((MARKS, MARKS), F32),
            vmem((2, DIM, MARKS), BF16),
            vmem((2, DIM, TOKENS), F32),
            vmem((2, TOKENS, DIM), F32),
            vmem((16, DIM), F32),
            vmem((NY - 1, 16, DIM), F32),
            vmem((rows, DIM), BF16),
            pltpu.SemaphoreType.DMA((7,)),
            pltpu.SemaphoreType.DMA((13,)),
            pltpu.SemaphoreType.DMA((13,)),
        ],
        compiler_params=pltpu.CompilerParams(
            collective_id=0, has_side_effects=True, vmem_limit_bytes=56 * 1024 * 1024
        ),
    )(*args, gain)
    return out.reshape(TOKENS, 2, DIM)


def solution(mesh):
    spec = P("seq", "head", None)
    return jax.shard_map(
        on_device,
        mesh=mesh,
        in_specs=(spec, spec, spec, P("head", None)),
        out_specs=spec,
        check_vma=False,
    )
```

time: 63.1 us -> 50.8 us (0.81)
  Pallas kernels: 60.4 us -> 48.1 us
    pallas_call x1, Pallas kernels: 60.4 us -> 48.1 us  [on_device(): pl.pallas_call(kernel, out_shape=jax.ShapeDtypeStruct((rows, DIM), BF16),...]
where the time goes in v2:
time: 50.8 us; the launch traced here: 50.7 us
  Pallas kernels  48.1 us (95%)
  local copies, waits for them, and re-layouts  2.58 us (5%)
    pallas_call x1, Pallas kernels, on_device(): pl.pallas_call(kernel, out_shape=jax.ShapeDtypeStruct((rows, DIM), BF16),...  48.1 us
    unnamed x1, local copies, waits for them, and re-layouts  2.58 us

profile of v2, /device:TPU:1, one launch (start us, length us, event | category | flops | bytes accessed | tf_op | source)
XLA Modules:
  0.0 50.7 jit_solution(14797776924400531701)
XLA Ops:
  0.0 48.1 %shard_map.46 = bf16[4096,128]{1,0:T(8,128)(2,1)} custom-call(bf16[4096,128]{1,0:T(8,128)(2,1)} %bitcast.5, bf16[4096,128]{1,0:T(8,128)(2,1)} %bitcast.6, bf16[4096,128]{1,0:T(8,128)(2,1)} %bitcast.7, f32[2,128]{1,0:T(2,128)} %gain_ref.1), custom_call_target="tpu_custom_call" | custom-call | tf_op jit(solution)/shard_map/pallas_call | solution.py:283
  48.1 2.6 %copy.6 = bf16[2048,2,128]{2,1,0:T(2,128)(2,1)} copy(bf16[2048,2,128]{2,1,0:T(2,128)(2,1)} %bitcast.4) | data formatting | bytes 2097152

commit v3 on v2

--- a/solution.py
+++ b/solution.py
@@ -203,12 +203,9 @@
     t0[...] = dot3(a2, a2, NT) * shrink
     p0 = split(t0[...])
     t1[...] = dot3(p0, p0)
-    s2 = split(t1[...])
-    t2[...] = dot3(s2, p0)
-    w_ref[...] = eye_times(13.0) - 15.0 * t0[...] + 7.0 * t1[...] - t2[...]
+    cube = dot(t1[...].astype(BF16), p0[0])
+    w_ref[...] = eye_times(13.0) - 15.0 * t0[...] + 7.0 * t1[...] - cube
     t2[...] = 0.25 * dot3(p0, split(w_ref[...]))
-    p1 = split(t2[...])
-    t0[...] = dot3(p1, p1)
 
     arrived(reduce_copies)
     own_log, far_logs = logs[x], rlogs[...]
@@ -219,7 +216,10 @@
     kvt[x, z] = (value * (1.0 / total)).astype(BF16)
     kv_copies = spread(kvt.at[x, z])
 
-    t1[...] = eye_times(13.0) - 15.0 * t2[...] + dot3(split(t0[...]), split(eye_times(7.0) - t2[...]))
+    p1 = split(t2[...])
+    t0[...] = dot3(p1, p1)
+    cube = dot(t0[...].astype(BF16), p1[0])
+    t1[...] = eye_times(13.0) - 15.0 * t2[...] + 7.0 * t0[...] - cube
     w_ref[...] = dot3(split(w_ref[...]), split(t1[...])) * (shrink * 0.0625)
 
     def query_weights(h, _):

time: 50.8 us -> 46.9 us (0.923)
  Pallas kernels: 48.1 us -> 44.2 us
    pallas_call x1, Pallas kernels: 48.1 us -> 44.2 us  [on_device(): pl.pallas_call(kernel, out_shape=jax.ShapeDtypeStruct((rows, DIM), BF16),...]
where the time goes in v3:
time: 46.9 us; the launch traced here: 46.7 us
  Pallas kernels  44.2 us (94%)
  local copies, waits for them, and re-layouts  2.58 us (6%)
    pallas_call x1, Pallas kernels, on_device(): pl.pallas_call(kernel, out_shape=jax.ShapeDtypeStruct((rows, DIM), BF16),...  44.2 us
    unnamed x1, local copies, waits for them, and re-layouts  2.58 us

profile of v3, /device:TPU:1, one launch (start us, length us, event | category | flops | bytes accessed | tf_op | source)
XLA Modules:
  0.0 46.7 jit_solution(9823331172668407451)
XLA Ops:
  0.0 44.2 %shard_map.46 = bf16[4096,128]{1,0:T(8,128)(2,1)} custom-call(bf16[4096,128]{1,0:T(8,128)(2,1)} %bitcast.5, bf16[4096,128]{1,0:T(8,128)(2,1)} %bitcast.6, bf16[4096,128]{1,0:T(8,128)(2,1)} %bitcast.7, f32[2,128]{1,0:T(2,128)} %gain_ref.1), custom_call_target="tpu_custom_call" | custom-call | tf_op jit(solution)/shard_map/pallas_call | solution.py:283
  44.2 2.6 %copy.6 = bf16[2048,2,128]{2,1,0:T(2,128)(2,1)} copy(bf16[2048,2,128]{2,1,0:T(2,128)(2,1)} %bitcast.4) | data formatting | bytes 2097152

commit v4 on v3

--- a/solution.py
+++ b/solution.py
@@ -1,3 +1,5 @@
+import functools
+
 import jax
 import jax.numpy as jnp
 from jax import lax
@@ -42,10 +44,10 @@
 
 
 def kernel(
-    q_hbm, k_hbm, v_hbm, gain_ref, o_hbm,
-    xq, xk, xv, qh, kh, vh, marks, gq, gk, mq, mk, wide,
+    q_hbm, k_hbm, v_hbm, gain_hbm, att, factors,
+    xq, xk, xv, gain_ref, qh, kh, vh, marks, gq, gk, mq, mk, wide,
     away, rcore, parts, logs, rparts, rlogs, kvt, kvf, weights_f, totals,
-    t0, t1, t2, w_ref, mixt, attt, att, sqs, sqr, out,
+    t0, t1, t2, w_ref, mixt, attt, sqs, sqr,
     local_sem, ssem, rsem,
 ):
     s = lax.axis_index("seq")
@@ -94,7 +96,7 @@
 
     loads = [
         pltpu.make_async_copy(src, dst, local_sem.at[i])
-        for i, (src, dst) in enumerate(((q_hbm, xq), (k_hbm, xk), (v_hbm, xv)))
+        for i, (src, dst) in enumerate(((q_hbm, xq), (k_hbm, xk), (v_hbm, xv), (gain_hbm, gain_ref)))
     ]
     for load in loads:
         load.start()
@@ -140,6 +142,7 @@
     k_copies = spread(gk.at[c, x, z])
     head_rows(xk, kh)
     loads[2].wait()
+    loads[3].wait()
     head_rows(xv, vh)
     head_rows(xq, qh)
     arrived(q_copies)
@@ -255,40 +258,43 @@
             att[h, pl.ds(n * 128, 128), :] = attt[h, :, 128 * n : 128 * n + 128].T * gain_ref[h : h + 1, :]
     arrived(y_copies)
     total = sqs[...] + sqr[0] + sqr[1] + sqr[2]
-    factors = lax.rsqrt(total * (1.0 / (8 * DIM)) + EPSILON)
-
-    stores = []
-    for n in range(TOKENS // 128):
-        rows = pl.ds(n * 128, 128)
-        factor = jnp.broadcast_to(factors[n : n + 1, :], (DIM, DIM)).T
-        for h in range(2):
-            wide[pl.ds(n * 256 + h, 128, stride=2), :] = att[h, rows, :] * factor
-        cut = pl.ds(n * 256, 256)
-        out[cut, :] = wide[cut, :].astype(BF16)
-        if n % 4 == 3:
-            cut = pl.ds((n - 3) * 256, 1024)
-            store = pltpu.make_async_copy(out.at[cut], o_hbm.at[cut], local_sem.at[3 + n // 4])
-            store.start()
-            stores.append(store)
+    factors[...] = lax.rsqrt(total * (1.0 / (8 * DIM)) + EPSILON)
     for copy in started:
         copy.wait_send()
+
+
+def finish(att, factors, o_hbm, wide, out, out_sem):
+    steps = 4
+    tokens = TOKENS // steps
+    stores = []
+    for n in range(steps):
+        for i in range(n * tokens // DIM, (n + 1) * tokens // DIM):
+            factor = jnp.broadcast_to(factors[i : i + 1, :], (DIM, DIM)).T
+            for h in range(2):
+                wide[pl.ds(2 * DIM * i + h, DIM, stride=2), :] = att[h, pl.ds(DIM * i, DIM), :] * factor
+        cut = pl.ds(n * 2 * tokens, 2 * tokens)
+        out[cut, :] = wide[cut, :].astype(BF16)
+        stores.append(pltpu.make_async_copy(out.at[cut], o_hbm.at[cut], out_sem.at[n]))
+        stores[n].start()
     for store in stores:
         store.wait()
 
 
 def on_device(queries, key_rows, values, gain):
     rows = 2 * TOKENS
-    args = [a.reshape(rows, DIM) for a in (queries, key_rows, values)]
+    args = [a.reshape(rows, DIM) for a in (queries, key_rows, values)] + [gain]
+    args = [pltpu.with_memory_space_constraint(a, pltpu.HBM) for a in args]
     vmem = pltpu.VMEM
-    out = pl.pallas_call(
+    att, factors = pl.pallas_call(
         kernel,
-        out_shape=jax.ShapeDtypeStruct((rows, DIM), BF16),
-        in_specs=[pl.BlockSpec(memory_space=pl.ANY)] * 3 + [pl.BlockSpec(memory_space=pltpu.VMEM)],
-        out_specs=pl.BlockSpec(memory_space=pl.ANY),
+        out_shape=(jax.ShapeDtypeStruct((2, TOKENS, DIM), F32), jax.ShapeDtypeStruct((16, DIM), F32)),
+        in_specs=[pl.BlockSpec(memory_space=pltpu.HBM)] * 4,
+        out_specs=(pl.BlockSpec(memory_space=pltpu.VMEM), pl.BlockSpec(memory_space=pltpu.VMEM)),
         scratch_shapes=[
             vmem((rows, DIM), BF16),
             vmem((rows, DIM), BF16),
             vmem((rows, DIM), BF16),
+            vmem((2, DIM), F32),
             vmem((2, TOKENS, DIM), BF16),
             vmem((2, TOKENS, DIM), BF16),
             vmem((2, TOKENS, DIM), BF16),
@@ -297,7 +303,7 @@
             vmem((NC, NX, NZ, 16, DIM), BF16),
             vmem((2, 2, MARKS // 2, DIM), BF16),
             vmem((2, 2, MARKS // 2, DIM), BF16),
-            vmem((rows, DIM), F32),
+            vmem((512, DIM), F32),
             vmem((2, 2, MARKS // 2, DIM), F32),
             vmem((2, 2, MARKS // 2, DIM), F32),
             vmem((NX, NZ, 16, DIM), BF16),
@@ -314,18 +320,28 @@
             vmem((MARKS, MARKS), F32),
             vmem((2, DIM, MARKS), BF16),
             vmem((2, DIM, TOKENS), F32),
-            vmem((2, TOKENS, DIM), F32),
             vmem((16, DIM), F32),
             vmem((NY - 1, 16, DIM), F32),
-            vmem((rows, DIM), BF16),
-            pltpu.SemaphoreType.DMA((7,)),
+            pltpu.SemaphoreType.DMA((4,)),
             pltpu.SemaphoreType.DMA((13,)),
             pltpu.SemaphoreType.DMA((13,)),
         ],
         compiler_params=pltpu.CompilerParams(
-            collective_id=0, has_side_effects=True, vmem_limit_bytes=56 * 1024 * 1024
+            collective_id=0, has_side_effects=True, vmem_limit_bytes=40 * 1024 * 1024
         ),
-    )(*args, gain)
+    )(*args)
+    out = pl.pallas_call(
+        finish,
+        out_shape=jax.ShapeDtypeStruct((rows, DIM), BF16),
+        in_specs=[pl.BlockSpec(memory_space=pltpu.VMEM)] * 2,
+        out_specs=pl.BlockSpec(memory_space=pl.ANY),
+        scratch_shapes=[
+            vmem((rows, DIM), F32),
+            vmem((rows, DIM), BF16),
+            pltpu.SemaphoreType.DMA((4,)),
+        ],
+        compiler_params=pltpu.CompilerParams(vmem_limit_bytes=16 * 1024 * 1024),
+    )(att, factors)
     return out.reshape(TOKENS, 2, DIM)
 
 

time: 46.9 us -> 43.6 us (0.930)
  local copies, waits for them, and re-layouts: 2.58 us -> 0 us
  Pallas kernels: 44.2 us -> 43.5 us
    unnamed x1 -> x0, local copies, waits for them, and re-layouts: 2.58 us -> none
    pallas_call x1 -> x2, Pallas kernels: 44.2 us -> 43.5 us  [the longest x1 42.3 us: on_device(): pl.pallas_call(kernel, out_shape=(jax.ShapeDtypeStruct((2, TOKENS, DIM),...]
where the time goes in v4:
time: 43.6 us
  Pallas kernels  43.5 us (100%)
    pallas_call x1, Pallas kernels, on_device(): pl.pallas_call(kernel, out_shape=(jax.ShapeDtypeStruct((2, TOKENS, DIM),...  42.3 us
    pallas_call x1, Pallas kernels, on_device(): pl.pallas_call(finish, out_shape=jax.ShapeDtypeStruct((rows, DIM), BF16),...  1.21 us

profile of v4, /device:TPU:1, one launch (start us, length us, event | category | flops | bytes accessed | tf_op | source)
XLA Modules:
  0.0 43.6 jit_solution(5878783190232610171)
XLA Ops:
  0.0 42.3 %shard_map.46 = (f32[2,2048,128]{2,1,0:T(8,128)S(1)}, f32[16,128]{1,0:T(8,128)S(1)}) custom-call(bf16[4096,128]{1,0:T(8,128)(2,1)} %bitcast.4, bf16[4096,128]{1,0:T(8,128)(2,1)} %bitcast.5, bf16[4096,128]{1,0:T(8,128)(2,1)} %bitcast.6, f32[2,128]{1,0:T(2,128)} %gain_hbm.1), custom_call_target="tpu_custom_call" | custom-call | tf_op jit(solution)/shard_map/pallas_call | solution.py:288
  42.3 1.2 %shard_map.47 = bf16[4096,128]{1,0:T(8,128)(2,1)} custom-call(f32[2,2048,128]{2,1,0:T(8,128)S(1)} %get-tuple-element.7.att, f32[16,128]{1,0:T(8,128)S(1)} %get-tuple-element.8.factors), custom_call_target="tpu_custom_call" | custom-call | tf_op jit(solution)/shard_map/pallas_call | solution.py:333

commit v5 on v4

--- a/solution.py
+++ b/solution.py
@@ -1,5 +1,3 @@
-import functools
-
 import jax
 import jax.numpy as jnp
 from jax import lax
@@ -98,13 +96,12 @@
         pltpu.make_async_copy(src, dst, local_sem.at[i])
         for i, (src, dst) in enumerate(((q_hbm, xq), (k_hbm, xk), (v_hbm, xv), (gain_hbm, gain_ref)))
     ]
-    for load in loads:
-        load.start()
-
     barrier = pltpu.get_barrier_semaphore()
     peers = [chip(d) for d in PEERS] + [sibling] + [at_y(d) for d in range(1, NY)]
     for peer in peers:
         pl.semaphore_signal(barrier, inc=1, device_id=peer, device_id_type=MESH)
+    for load in loads:
+        load.start()
 
     def means(src, dst):
         for j in range(TOKENS // SEGMENT):
@@ -139,7 +136,8 @@
     q_copies = spread(gq.at[c, x, z])
     loads[1].wait()
     means(xk, gk)
-    k_copies = spread(gk.at[c, x, z])
+    block = gk.at[c, x, z]
+    k_copies = [send_all([(block, block, (d, 0)) for d in (4, 3, 5, 2, 6, 1, 7)], rparts.at[pl.ds(0, NZ - 1)])]
     head_rows(xk, kh)
     loads[2].wait()
     loads[3].wait()
@@ -147,6 +145,9 @@
     head_rows(xq, qh)
     arrived(q_copies)
     q_copies = [send(gq.at[c], gq.at[c], sibling)]
+    arrived(k_copies)
+    column = gk.at[c, x]
+    k_copies = [send_all([(column, column, (0, d)) for d in (2, 1, 3)], rparts.at[pl.ds(0, (NX - 1) * NZ)])]
     landmarks(gq, mq, c)
 
     def local_part(h, rows):
@@ -167,9 +168,9 @@
     arrived(q_copies)
     landmarks(gq, mq, other)
     part_away(other)
+    value, log_sum = local_part(c, mq[c].reshape(MARKS, DIM))
     arrived(k_copies)
     k_copies = [send(gk.at[c], gk.at[c], sibling)]
-    value, log_sum = local_part(c, mq[c].reshape(MARKS, DIM))
     arrived(core_copies)
     far = jnp.concatenate([rcore[0, 0], rcore[1, 0]], axis=0)
     far_log = jnp.concatenate([rcore[0, 1], rcore[1, 1]], axis=0)
@@ -303,7 +304,7 @@
             vmem((NC, NX, NZ, 16, DIM), BF16),
             vmem((2, 2, MARKS // 2, DIM), BF16),
             vmem((2, 2, MARKS // 2, DIM), BF16),
-            vmem((512, DIM), F32),
+            vmem((520, DIM), F32),
             vmem((2, 2, MARKS // 2, DIM), F32),
             vmem((2, 2, MARKS // 2, DIM), F32),
             vmem((NX, NZ, 16, DIM), BF16),
@@ -323,8 +324,8 @@
             vmem((16, DIM), F32),
             vmem((NY - 1, 16, DIM), F32),
             pltpu.SemaphoreType.DMA((4,)),
-            pltpu.SemaphoreType.DMA((13,)),
-            pltpu.SemaphoreType.DMA((13,)),
+            pltpu.SemaphoreType.DMA((14,)),
+            pltpu.SemaphoreType.DMA((14,)),
         ],
         compiler_params=pltpu.CompilerParams(
             collective_id=0, has_side_effects=True, vmem_limit_bytes=40 * 1024 * 1024
@@ -336,7 +337,7 @@
         in_specs=[pl.BlockSpec(memory_space=pltpu.VMEM)] * 2,
         out_specs=pl.BlockSpec(memory_space=pl.ANY),
         scratch_shapes=[
-            vmem((rows, DIM), F32),
+            vmem((rows + 8, DIM), F32),
             vmem((rows, DIM), BF16),
             pltpu.SemaphoreType.DMA((4,)),
         ],

time: 43.6 us -> 43.6 us (level)
  no operation moved by 1% of the time
where the time goes in v5:
time: 43.6 us; the launch traced here: 43.5 us
  Pallas kernels  43.5 us (100%)
    pallas_call x1, Pallas kernels, on_device(): pl.pallas_call(kernel, out_shape=(jax.ShapeDtypeStruct((2, TOKENS, DIM),...  42.3 us
    pallas_call x1, Pallas kernels, on_device(): pl.pallas_call(finish, out_shape=jax.ShapeDtypeStruct((rows, DIM), BF16),...  1.21 us

profile of v5, /device:TPU:1, one launch (start us, length us, event | category | flops | bytes accessed | tf_op | source)
XLA Modules:
  0.0 43.5 jit_solution(11247094242807521668)
XLA Ops:
  0.0 42.3 %shard_map.46 = (f32[2,2048,128]{2,1,0:T(8,128)S(1)}, f32[16,128]{1,0:T(8,128)S(1)}) custom-call(bf16[4096,128]{1,0:T(8,128)(2,1)} %bitcast.4, bf16[4096,128]{1,0:T(8,128)(2,1)} %bitcast.5, bf16[4096,128]{1,0:T(8,128)(2,1)} %bitcast.6, f32[2,128]{1,0:T(2,128)} %gain_hbm.1), custom_call_target="tpu_custom_call" | custom-call | tf_op jit(solution)/shard_map/pallas_call | solution.py:289
  42.3 1.2 %shard_map.47 = bf16[4096,128]{1,0:T(8,128)(2,1)} custom-call(f32[2,2048,128]{2,1,0:T(8,128)S(1)} %get-tuple-element.7.att, f32[16,128]{1,0:T(8,128)S(1)} %get-tuple-element.8.factors), custom_call_target="tpu_custom_call" | custom-call | tf_op jit(solution)/shard_map/pallas_call | solution.py:334
